TPU v7x, 256 devices: a whole 4x4x8 slice. The times are simulated.
256 devices in a mesh: dp: 32 (over z, x), tensor: 8 (over y, core).
Axes of the slice: x: 4, y: 4, z: 8, core: 2. Of those that a mesh axis runs over, the one named last changes fastest.
Arguments:
- activations: bfloat16 [28672, 4096], P('dp', 'tensor'), may hold values from -6 to 6
- out_grads: bfloat16 [28672, 4096], P('dp', 'tensor'), may hold values from -6 to 6
- gate_act: bfloat16 [28672, 14336], P('dp', 'tensor'), may hold values from -6 to 6
- w_down: bfloat16 [14336, 4096], P('tensor', 'dp'), may hold values from -0.09375 to 0.09375
- proj_in: bfloat16 [4096, 64], P('tensor'), may hold values from -0.09375 to 0.09375
- proj_out: bfloat16 [14336, 64], P('tensor'), may hold values from -0.046875 to 0.046875
- lengths: int32 [32, 8], P('dp'), may hold values from 1 to 448, 896 in all within a row
- assign: int32 [256], replicated, may hold values from 0 to 255, each once
Outputs:
- loggrads: float32 [256, 64, 64], P('dp', 'tensor')
Inputs may be any that keep to these rules, and one draw needn't show every extreme that they name: `lengths`: each row gives the token counts of the 8 sequences packed into one data group's 896 rows and sums to 896. `assign`: a permutation of the sequence numbers.
All inputs are finite; a program needn't handle non-finite values.
Results may differ from a plain program's by a relative error of at most 0.013.
Values may be sent and summed in bfloat16 or wider, within the bound.
No kernel may reach another device: no remote copies, remote signals or barrier semaphores. Data moves between devices by JAX's collectives and lax.ppermute only.
A program may use at most 128 MiB of HBM per device.

v0:
```python
import jax
import jax.numpy as jnp
from jax import lax
from jax.sharding import PartitionSpec as P


def shards(activations, out_grads, gate_act, w_down, proj_in, proj_out, lengths, assign):
    tok_rows = activations.shape[0]
    rank_all = proj_in.shape[1]
    full_grads = lax.all_gather(out_grads, "tensor", axis=1, tiled=True)
    hidden_grad = lax.dot_general(
        full_grads,
        lax.all_gather(w_down, "dp", axis=1, tiled=True),
        (((1,), (1,)), ((), ())),
        preferred_element_type=jnp.float32,
    )
    up_grad = (hidden_grad * gate_act.astype(jnp.float32)).astype(jnp.bfloat16)
    out_part = jnp.dot(up_grad, proj_out, preferred_element_type=jnp.float32)
    in_part = jnp.dot(activations, proj_in, preferred_element_type=jnp.float32)
    col_count = rank_all // lax.axis_size("tensor")
    shard_index = lax.axis_index("tensor")
    in_sum, out_sum = lax.psum((in_part, out_part), "tensor")
    in_mine = lax.dynamic_slice_in_dim(in_sum, shard_index * col_count, col_count, 1)
    seq_lengths = lengths[0]
    seq_ends = jnp.cumsum(seq_lengths)
    starts = seq_ends - seq_lengths
    positions = lax.iota(jnp.int32, tok_rows)
    inside = (positions[None, :] >= starts[:, None]) & (positions[None, :] < seq_ends[:, None])
    member = jnp.where(inside, 1.0 / seq_lengths[:, None].astype(jnp.float32), 0.0)
    weighted = member[:, :, None] * in_mine[None, :, :]
    result = jnp.einsum("ctp,tq->cpq", weighted, out_sum, precision=lax.Precision.HIGHEST)
    per_group = seq_lengths.shape[0]
    group_count = lax.axis_size("dp")
    seq_total = per_group * group_count
    group_index = lax.axis_index("dp")
    mine_ids = lax.dynamic_slice_in_dim(assign, group_index * per_group, per_group, 0)
    placing = (mine_ids[None, :] == lax.iota(jnp.int32, seq_total)[:, None]).astype(jnp.float32)
    flat_result = result.reshape(per_group, col_count * rank_all)
    spread = jnp.dot(placing, flat_result, precision=lax.Precision.HIGHEST)
    owned = lax.psum_scatter(
        spread.astype(jnp.bfloat16), "dp", scatter_dimension=0, tiled=True
    ).astype(jnp.float32)
    return owned.reshape(per_group, col_count, rank_all)


def solution(mesh):
    in_specs = (
        P("dp", "tensor"),
        P("dp", "tensor"),
        P("dp", "tensor"),
        P("tensor", "dp"),
        P("tensor", None),
        P("tensor", None),
        P("dp", None),
        P(),
    )
    out_specs = P("dp", "tensor", None)
    return jax.shard_map(shards, mesh=mesh, in_specs=in_specs, out_specs=out_specs, check_vma=False)
```

profile of v0, /device:TPU:8, one launch (start us, length us, event | category | flops | bytes accessed | tf_op | source)
XLA Modules:
  0.0 511.5 jit_solution(17634856475808253684)
XLA Ops:
  6.5 0.7 all-gather.3.cloned.1.call-update
  7.3 0.0 all-gather.5.cloned.1.call-start
  7.3 0.7 all-gather.5.cloned.1.call-update
  8.0 0.0 all-reduce.3.cloned.1.call-start
  8.1 0.8 reduce-window.7
  8.9 0.7 bitcast_subtract_fusion
  9.5 0.0 copy-done
  9.5 2.0 fusion.10
  11.5 47.6 %all-gather.3.cloned.1.call-done = bf16[896,4096]{1,0:T(8,128)(2,1)} async-done(((bf16[896,512]{1,0:T(8,128)(2,1)}), bf16[896,4096]{1,0:T(8,128)(2,1)}) %all-gather.3.cloned.1.call-update) | async-done | bytes 7340048 | tf_op jit(solution)/shard_map/all_gather | solution.py:10
  59.1 142.3 %all-gather.5.cloned.1.call-done = bf16[1792,4096]{1,0:T(8,128)(2,1)} async-done(((bf16[1792,128]{1,0:T(8,128)(2,1)}), bf16[1792,4096]{1,0:T(8,128)(2,1)}) %all-gather.5.cloned.1.call-update) | async-done | bytes 14680080 | tf_op jit(solution)/shard_map/all_gather | solution.py:13
  201.4 23.2 %fusion = f32[896,64]{0,1:T(8,128)} fusion(bf16[1792,64]{0,1:T(8,128)(2,1)} %param.13, bf16[896,1792]{1,0:T(8,128)(2,1)} %param.10, bf16[896,4096]{1,0:T(8,128)(2,1)} %all-gather.3.cloned.1.call-done, bf16[1792,4096]{1,0:T(8,128)(2,1)} %all-gather.5.cloned.1.call-done), kind=kOutput, calls=%fused_computation.1 | convolution fusion | flops 13363675136 | bytes 25690112 | tf_op jit(solution)/shard_map/dot_general | solution.py:18
  224.6 0.0 all-reduce.3.cloned.1.call-update
  224.7 0.0 reduce-scatter.2.cloned.1.call-start
  224.7 0.0 copy-done.2
  224.8 0.1 dynamic_slice.6
  224.8 0.1 fusion.8
  224.9 60.4 %all-reduce.3.cloned.1.call-done = (f32[896,64]{0,1:T(8,128)}, f32[896,64]{0,1:T(8,128)}) async-done(((f32[896,64]{0,1:T(8,128)}, f32[896,64]{0,1:T(8,128)}), (f32[896,64]{0,1:T(8,128)}, f32[896,64]{0,1:T(8,128)})) %all-reduce.3.cloned.1.call-update) | async-done | bytes 458768 | tf_op jit(solution)/shard_map/psum | solution.py:22
  285.3 0.8 constant_dynamic-slice_fusion
  286.1 1.3 fusion.1
  287.4 0.1 reshape.108
  287.5 1.0 convolution_convert_fusion
  288.5 0.0 reduce-scatter.2.cloned.1.call-update
  288.5 215.0 %reduce-scatter.2.cloned.1.call-done = bf16[8,512]{1,0:T(8,128)(2,1)} async-done(((bf16[256,512]{1,0:T(8,128)(2,1)}), bf16[8,512]{1,0:T(8,128)(2,1)}) %reduce-scatter.2.cloned.1.call-update) | async-done | bytes 8208 | tf_op jit(solution)/shard_map/reduce_scatter | solution.py:40
  503.6 1.4 reshape.112
  (6 shorter events, 0.0 us)
Async XLA Ops:
  6.5 3.0 copy-start
  6.5 52.6 %all-gather.3.cloned.1.call-start = ((), (), s32[]{:S(2)}) async-start(), calls=%async_computation.1 | async-start | bytes 8257536 | tf_op jit(solution)/shard_map/all_gather | solution.py:10
  7.3 194.2 %all-gather.5.cloned.1.call-start = ((), (), s32[]{:S(2)}) async-start(), calls=%async_computation.2 | async-start | bytes 15138816 | tf_op jit(solution)/shard_map/all_gather | solution.py:13
  8.0 277.3 %all-reduce.3.cloned.1.call-start = ((), (), s32[]{:S(2)}) async-start(), calls=%async_computation.4 | async-start | bytes 917504 | tf_op jit(solution)/shard_map/psum | solution.py:22
  11.5 213.2 %copy-start.2 = (s32[1,8]{1,0:T(1,128)S(1)}, s32[1,8]{1,0:T(1,128)}, u32[]{:S(2)}) copy-start(s32[1,8]{1,0:T(1,128)} %param.14) | copy-start | bytes 100
  11.5 213.2 %copy-start.1 = (s32[256]{0:T(256)S(1)}, s32[256]{0:T(256)}, u32[]{:S(2)}) copy-start(s32[256]{0:T(256)} %param.15) | copy-start | bytes 3076
  224.7 278.9 %reduce-scatter.2.cloned.1.call-start = ((), (), s32[]{:S(2)}) async-start(), calls=%async_computation.3 | async-start | bytes 270336 | tf_op jit(solution)/shard_map/reduce_scatter | solution.py:40
Sparse Core Ops, SparseCore 0:
  9.2 49.8 all-gather.2
  61.6 139.7 all-gather.4
  224.8 60.4 all-reduce.2
  289.5 214.0 reduce-scatter.1
where the time goes:
time: 512 us; the launch traced here: 511 us
  waiting for transfers between devices  467 us (91%)
  matrix products  27.5 us (5%)
  between operations  13.2 us (3%)
    reduce_scatter x1, waiting for transfers between devices, shards(): lax.psum_scatter(spread.astype(jnp.bfloat16), 'dp', scatter_dimension=0,...  215 us
    all_gather x1, waiting for transfers between devices, shards(): lax.all_gather(w_down, 'dp', axis=1, tiled=True)  142 us
    psum x1, waiting for transfers between devices, shards(): in_sum, out_sum = lax.psum((in_part, out_part), 'tensor')  60.4 us
    all_gather x1, waiting for transfers between devices, shards(): full_grads = lax.all_gather(out_grads, 'tensor', axis=1, tiled=True)  47.6 us
    dot_general x1, matrix products, shards(): out_part = jnp.dot(up_grad, proj_out, preferred_element_type=jnp.float32)  23.2 us
  transfers between devices with their start and end apart: 4, of which 4 were waited for; matrix products, arithmetic and copies ran while one was open for 1% of the time, Pallas kernels for 0%

commit v1 on v0

--- a/solution.py
+++ b/solution.py
@@ -4,10 +4,32 @@
 from jax.sharding import PartitionSpec as P
 
 
+def ends_handle(message, axis_k):
+    block_next = list(message.shape[1:])
+    block_next[axis_k] *= message.shape[0]
+    return jnp.moveaxis(message, 0, axis_k).reshape(block_next)
+
+
+def keys_watch(unit, row_axis, d_out=1):
+    n = lax.psum(1, row_axis)
+    found = list(map(lambda p: (p, (p + 1) % n), range(n)))
+    e_now, next_value = ([], [])
+    crops = [(it, j0) for j0, it in found]
+    for dd in range(n - 1):
+        if dd % 2 == 0:
+            e_now.append(lax.ppermute(e_now[-1] if e_now else unit, row_axis, found))
+        else:
+            next_value.append(lax.ppermute(next_value[-1] if next_value else unit, row_axis, crops))
+    carry_in = jnp.stack([*e_now[::-1], unit, *next_value])
+    part_now = lax.axis_index(row_axis) - len(e_now)
+    carry_in = carry_in[(jnp.arange(n) - part_now) % n]
+    return ends_handle(carry_in, d_out)
+
+
 def shards(activations, out_grads, gate_act, w_down, proj_in, proj_out, lengths, assign):
     tok_rows = activations.shape[0]
     rank_all = proj_in.shape[1]
-    full_grads = lax.all_gather(out_grads, "tensor", axis=1, tiled=True)
+    full_grads = keys_watch(out_grads, "tensor")
     hidden_grad = lax.dot_general(
         full_grads,
         lax.all_gather(w_down, "dp", axis=1, tiled=True),

time: 512 us -> 462 us (0.902)
  waiting for transfers between devices: 467 us -> 378 us
  local copies, waits for them, and re-layouts: 2.3 us -> 36 us
  starting transfers between devices: 0.12 us -> 5.33 us
    all_gather x1, waiting for transfers between devices: 142 us -> 58.4 us  [shards(): lax.all_gather(w_down, 'dp', axis=1, tiled=True)]
    all_gather x1 -> x0, waiting for transfers between devices: 47.6 us -> none  [shards(): full_grads = lax.all_gather(out_grads, 'tensor', axis=1, tiled=True)]
    ppermute x0 -> x7, waiting for transfers between devices: none -> 43.2 us  [the longest x4 43.2 us: keys_watch(): e_now.append(lax.ppermute(e_now[-1] if e_now else unit, row_axis, found))]
    unnamed x6 -> x19, local copies, waits for them, and re-layouts: 0.01 us -> 13.9 us
    transpose x0 -> x1, local copies, waits for them, and re-layouts: none -> 11.6 us  [ends_handle(): return jnp.moveaxis(message, 0, axis_k).reshape(block_next)]
    gather x0 -> x1, local copies, waits for them, and re-layouts: none -> 7.2 us  [keys_watch(): carry_in = carry_in[(jnp.arange(n) - part_now) % n]]
    ppermute x0 -> x7, starting transfers between devices: none -> 5.25 us  [the longest x3 5.23 us: keys_watch(): lax.ppermute(next_value[-1] if next_value else unit, row_axis, crops)]
  transfers between devices with their start and end apart: 4 -> 10, of which waited for: 4 -> 7; matrix products, arithmetic and copies ran while one was open for 1% -> 8% of each run, Pallas kernels for 0% -> 0%
where the time goes in v1:
time: 462 us; the launch traced here: 461 us
  waiting for transfers between devices  378 us (82%)
  local copies, waits for them, and re-layouts  36 us (8%)
  matrix products  27.1 us (6%)
  between operations  13.2 us (3%)
  starting transfers between devices  5.33 us (1%)
    reduce_scatter x1, waiting for transfers between devices, shards(): lax.psum_scatter(spread.astype(jnp.bfloat16), 'dp', scatter_dimension=0,...  215 us
    psum x1, waiting for transfers between devices, shards(): in_sum, out_sum = lax.psum((in_part, out_part), 'tensor')  60.4 us
    all_gather x1, waiting for transfers between devices, shards(): lax.all_gather(w_down, 'dp', axis=1, tiled=True)  58.4 us
    ppermute x4, waiting for transfers between devices, keys_watch(): e_now.append(lax.ppermute(e_now[-1] if e_now else unit, row_axis, found))  43.2 us
    dot_general x1, matrix products, shards(): out_part = jnp.dot(up_grad, proj_out, preferred_element_type=jnp.float32)  22.7 us
    unnamed x19, local copies, waits for them, and re-layouts  13.9 us
    transpose x1, local copies, waits for them, and re-layouts, ends_handle(): return jnp.moveaxis(message, 0, axis_k).reshape(block_next)  11.6 us
  transfers between devices with their start and end apart: 10, of which 7 were waited for; matrix products, arithmetic and copies ran while one was open for 8% of the time, Pallas kernels for 0%

profile of v1, /device:TPU:8, one launch (start us, length us, event | category | flops | bytes accessed | tf_op | source)
XLA Modules:
  0.0 461.0 jit_solution(18018525603241624923)
XLA Ops:
  7.3 13.0 %collective-permute-done = bf16[896,512]{1,0:T(8,128)(2,1)S(1)} collective-permute-done((bf16[896,512]{1,0:T(8,128)(2,1)}, bf16[896,512]{1,0:T(8,128)(2,1)S(1)}, u32[]{:S(2)}, u32[]{:S(2)}) %collective-permute-start) | collective-permute-done | bytes 917536 | tf_op jit(solution)/shard_map/ppermute | solution.py:20
  20.4 1.7 collective-permute-start.4
  22.1 11.1 %collective-permute-done.1 = bf16[896,512]{1,0:T(8,128)(2,1)S(1)} collective-permute-done((bf16[896,512]{1,0:T(8,128)(2,1)S(1)}, bf16[896,512]{1,0:T(8,128)(2,1)S(1)}, u32[]{:S(2)}, u32[]{:S(2)}) %collective-permute-start.1) | collective-permute-done | bytes 917536 | tf_op jit(solution)/shard_map/ppermute | solution.py:20
  34.1 1.7 collective-permute-start.5
  35.8 11.2 %collective-permute-done.2 = bf16[896,512]{1,0:T(8,128)(2,1)} collective-permute-done((bf16[896,512]{1,0:T(8,128)(2,1)S(1)}, bf16[896,512]{1,0:T(8,128)(2,1)}, u32[]{:S(2)}, u32[]{:S(2)}) %collective-permute-start.2) | collective-permute-done | bytes 917536 | tf_op jit(solution)/shard_map/ppermute | solution.py:20
  48.5 2.0 fusion.12
  50.5 1.7 collective-permute-start.6
  52.2 7.9 %collective-permute-done.3 = bf16[896,512]{1,0:T(8,128)(2,1)} collective-permute-done((bf16[896,512]{1,0:T(8,128)(2,1)}, bf16[896,512]{1,0:T(8,128)(2,1)}, u32[]{:S(2)}, u32[]{:S(2)}) %collective-permute-start.3) | collective-permute-done | bytes 917536 | tf_op jit(solution)/shard_map/ppermute | solution.py:20
  60.2 2.2 bitcast_dynamic-update-slice_fusion.7
  62.3 2.2 bitcast_dynamic-update-slice_fusion.6
  64.5 2.2 bitcast_dynamic-update-slice_fusion.5
  66.7 1.0 bitcast_dynamic-update-slice_fusion.4
  68.7 2.2 bitcast_dynamic-update-slice_fusion.2
  70.9 2.2 bitcast_dynamic-update-slice_fusion.1
  73.1 1.0 bitcast_dynamic-update-slice_fusion
  74.1 7.2 %gather_fusion = bf16[8,896,512]{2,1,0:T(8,128)(2,1)} fusion(bf16[8,896,512]{2,1,0:T(8,128)(2,1)} %bitcast_dynamic-update-slice_fusion, s32[1024]{0:T(1024)S(1)} %pad_clamp_fusion), kind=kCustom, calls=%fused_computation | custom fusion | bytes 14680096 | tf_op jit(solution)/shard_map/gather | solution.py:25
  81.3 11.6 %copy.9 = bf16[896,8,512]{0,2,1:T(8,128)(2,1)} copy(bf16[896,8,512]{2,0,1:T(8,128)(2,1)} %bitcast.37) | data formatting | bytes 14680064 | tf_op jit(solution)/shard_map/transpose | solution.py:10
  92.9 58.4 %all-gather.2.cloned.1.call-done = bf16[1792,4096]{1,0:T(8,128)(2,1)} async-done(((bf16[1792,128]{1,0:T(8,128)(2,1)}), bf16[1792,4096]{1,0:T(8,128)(2,1)}) %all-gather.2.cloned.1.call-update) | async-done | bytes 14680080 | tf_op jit(solution)/shard_map/all_gather | solution.py:35
  151.4 22.7 %fusion = f32[896,64]{0,1:T(8,128)} fusion(bf16[1792,64]{0,1:T(8,128)(2,1)S(1)} %copy-done.3, bf16[896,1792]{1,0:T(8,128)(2,1)} %param.10, bf16[896,4096]{0,1:T(8,128)(2,1)} %bitcast.38, bf16[1792,4096]{1,0:T(8,128)(2,1)} %all-gather.2.cloned.1.call-done), kind=kOutput, calls=%fused_computation.2 | convolution fusion | flops 13363675136 | bytes 25690112 | tf_op jit(solution)/shard_map/dot_general | solution.py:40
  174.4 60.4 %all-reduce.3.cloned.1.call-done = (f32[896,64]{0,1:T(8,128)}, f32[896,64]{0,1:T(8,128)}) async-done(((f32[896,64]{0,1:T(8,128)}, f32[896,64]{0,1:T(8,128)}), (f32[896,64]{0,1:T(8,128)}, f32[896,64]{0,1:T(8,128)})) %all-reduce.3.cloned.1.call-update) | async-done | bytes 458768 | tf_op jit(solution)/shard_map/psum | solution.py:44
  235.5 1.3 fusion.1
  236.9 1.0 convolution_convert_fusion
  238.0 215.1 %reduce-scatter.2.cloned.1.call-done = bf16[8,512]{1,0:T(8,128)(2,1)} async-done(((bf16[256,512]{1,0:T(8,128)(2,1)}), bf16[8,512]{1,0:T(8,128)(2,1)}) %reduce-scatter.2.cloned.1.call-update) | async-done | bytes 8208 | tf_op jit(solution)/shard_map/reduce_scatter | solution.py:62
  453.1 1.4 reshape.165
  (35 shorter events, 5.3 us)
Async XLA Ops:
  6.5 42.0 %copy-start = (bf16[896,512]{1,0:T(8,128)(2,1)S(1)}, bf16[896,512]{1,0:T(8,128)(2,1)}, u32[]{:S(2)}) copy-start(bf16[896,512]{1,0:T(8,128)(2,1)} %param.8) | copy-start | bytes 2752516
  6.5 61.2 %copy-start.1 = (bf16[896,512]{1,0:T(8,128)(2,1)S(1)}, bf16[896,512]{1,0:T(8,128)(2,1)}, u32[]{:S(2)}) copy-start(bf16[896,512]{1,0:T(8,128)(2,1)} %param.9) | copy-start | bytes 2752516
  6.5 144.8 %all-gather.2.cloned.1.call-start = ((), (), s32[]{:S(2)}) async-start(), calls=%async_computation.1 | async-start | bytes 15138816 | tf_op jit(solution)/shard_map/all_gather | solution.py:35
  7.3 227.5 %all-reduce.3.cloned.1.call-start = ((), (), s32[]{:S(2)}) async-start(), calls=%async_computation.3 | async-start | bytes 917504 | tf_op jit(solution)/shard_map/psum | solution.py:44
  7.3 13.0 %collective-permute-start = (bf16[896,512]{1,0:T(8,128)(2,1)}, bf16[896,512]{1,0:T(8,128)(2,1)S(1)}, u32[]{:S(2)}, u32[]{:S(2)}) collective-permute-start(bf16[896,512]{1,0:T(8,128)(2,1)} %param.9), channel_id=1, source_target_pairs={{0,1},{1,2},{2,3},{3,4},{4,5},{5,6},{6,7},{7,0},{8,9},{9,10},{10,1... | collective-permute-start | bytes 2752520 | tf_op jit(solution)/shard_map/ppermute | solution.py:20
  20.3 12.8 %collective-permute-start.1 = (bf16[896,512]{1,0:T(8,128)(2,1)S(1)}, bf16[896,512]{1,0:T(8,128)(2,1)S(1)}, u32[]{:S(2)}, u32[]{:S(2)}) collective-permute-start(bf16[896,512]{1,0:T(8,128)(2,1)S(1)} %collective-permute-done), channel_id=1, source_target_pairs={{0,1},{1,2},{2,3},{3,4},{4,5},{5,6},{6,7},{7,0},{8,9},{9,10},{10,1... | collective-permute-start | bytes 2752520 | tf_op jit(solution)/shard_map/ppermute | solution.py:20
  20.4 13.7 %collective-permute-start.4 = (bf16[896,512]{1,0:T(8,128)(2,1)}, bf16[896,512]{1,0:T(8,128)(2,1)}, u32[]{:S(2)}, u32[]{:S(2)}) collective-permute-start(bf16[896,512]{1,0:T(8,128)(2,1)} %param.9), channel_id=1, source_target_pairs={{1,0},{2,1},{3,2},{4,3},{5,4},{6,5},{7,6},{0,7},{9,8},{10,9},{11,1... | collective-permute-start | bytes 2752520 | tf_op jit(solution)/shard_map/ppermute | solution.py:22
  33.2 0.9 copy-start.2
  34.1 12.9 %collective-permute-start.2 = (bf16[896,512]{1,0:T(8,128)(2,1)S(1)}, bf16[896,512]{1,0:T(8,128)(2,1)}, u32[]{:S(2)}, u32[]{:S(2)}) collective-permute-start(bf16[896,512]{1,0:T(8,128)(2,1)S(1)} %collective-permute-done.1), channel_id=1, source_target_pairs={{0,1},{1,2},{2,3},{3,4},{4,5},{5,6},{6,7},{7,0},{8,9},{9,10},{10,1... | collective-permute-start | bytes 2752520 | tf_op jit(solution)/shard_map/ppermute | solution.py:20
  34.1 16.4 %collective-permute-start.5 = (bf16[896,512]{1,0:T(8,128)(2,1)}, bf16[896,512]{1,0:T(8,128)(2,1)}, u32[]{:S(2)}, u32[]{:S(2)}) collective-permute-start(bf16[896,512]{1,0:T(8,128)(2,1)} %collective-permute-done.4), channel_id=1, source_target_pairs={{1,0},{2,1},{3,2},{4,3},{5,4},{6,5},{7,6},{0,7},{9,8},{10,9},{11,1... | collective-permute-start | bytes 2752520 | tf_op jit(solution)/shard_map/ppermute | solution.py:22
  47.0 13.1 %collective-permute-start.3 = (bf16[896,512]{1,0:T(8,128)(2,1)}, bf16[896,512]{1,0:T(8,128)(2,1)}, u32[]{:S(2)}, u32[]{:S(2)}) collective-permute-start(bf16[896,512]{1,0:T(8,128)(2,1)} %collective-permute-done.2), channel_id=1, source_target_pairs={{0,1},{1,2},{2,3},{3,4},{4,5},{5,6},{6,7},{7,0},{8,9},{9,10},{10,1... | collective-permute-start | bytes 2752520 | tf_op jit(solution)/shard_map/ppermute | solution.py:20
  50.5 22.6 %collective-permute-start.6 = (bf16[896,512]{1,0:T(8,128)(2,1)}, bf16[896,512]{1,0:T(8,128)(2,1)S(1)}, u32[]{:S(2)}, u32[]{:S(2)}) collective-permute-start(bf16[896,512]{1,0:T(8,128)(2,1)} %collective-permute-done.5), channel_id=1, source_target_pairs={{1,0},{2,1},{3,2},{4,3},{5,4},{6,5},{7,6},{0,7},{9,8},{10,9},{11,1... | collective-permute-start | bytes 2752520 | tf_op jit(solution)/shard_map/ppermute | solution.py:22
  81.3 70.1 %copy-start.3 = (bf16[1792,64]{0,1:T(8,128)(2,1)S(1)}, bf16[1792,64]{0,1:T(8,128)(2,1)}, u32[]{:S(2)}) copy-start(bf16[1792,64]{0,1:T(8,128)(2,1)} %param.13) | copy-start | bytes 688132
  151.4 22.8 %copy-start.5 = (s32[1,8]{1,0:T(1,128)S(1)}, s32[1,8]{1,0:T(1,128)}, u32[]{:S(2)}) copy-start(s32[1,8]{1,0:T(1,128)} %param.14) | copy-start | bytes 100
  151.4 22.9 %copy-start.4 = (s32[256]{0:T(256)S(1)}, s32[256]{0:T(256)}, u32[]{:S(2)}) copy-start(s32[256]{0:T(256)} %param.15) | copy-start | bytes 3076
  174.1 279.0 %reduce-scatter.2.cloned.1.call-start = ((), (), s32[]{:S(2)}) async-start(), calls=%async_computation.2 | async-start | bytes 270336 | tf_op jit(solution)/shard_map/reduce_scatter | solution.py:62
Sparse Core Ops, SparseCore 0:
  9.8 141.4 all-gather.1
  174.3 60.4 all-reduce.2
  239.1 213.9 reduce-scatter.1
